TPU v7x, 32 devices: a whole 2x2x4 slice. The times are simulated.
32 devices in a mesh: dp: 8 (over z, x), tensor: 4 (over y, core).
Axes of the slice: x: 2, y: 2, z: 4, core: 2. Of those that a mesh axis runs over, the one named last changes fastest.
Arguments:
- features: bfloat16 [8, 1500, 768], P('dp', 'tensor'), may hold values from -6 to 6
- cotangent: bfloat16 [8, 1500, 768], P('dp', 'tensor'), may hold values from -6 to 6
- w_query: bfloat16 [768, 768], P(None, 'tensor'), may hold values from -0.21875 to 0.21875
- bias_query: bfloat16 [768], P('tensor'), may hold values from -3 to 3
- w_key: bfloat16 [768, 768], P(None, 'tensor'), may hold values from -0.21875 to 0.21875
- w_value: bfloat16 [768, 768], P(None, 'tensor'), may hold values from -0.21875 to 0.21875
- bias_value: bfloat16 [768], P('tensor'), may hold values from -3 to 3
- w_out: bfloat16 [768, 768], P('tensor'), may hold values from -0.875 to 0.875
- bias_out: float32 [768], replicated, may hold values from -3 to 3
- norm1_gain: float32 [768], replicated, may hold values from 0.5 to 1.5
- norm1_bias: float32 [768], replicated, may hold values from -2 to 2
- norm2_gain: float32 [768], replicated, may hold values from 0.5 to 1.5
- norm2_bias: float32 [768], replicated, may hold values from -2 to 2
- w_fc1: bfloat16 [768, 3072], P(None, 'tensor'), may hold values from -0.21875 to 0.21875
- bias_fc1: bfloat16 [3072], P('tensor'), may hold values from -3 to 3
- w_fc2: bfloat16 [3072, 768], P('tensor'), may hold values from -0.21875 to 0.21875
- bias_fc2: float32 [768], replicated, may hold values from -3 to 3
Outputs:
- layer_out: bfloat16 [8, 1500, 768], P('dp', 'tensor')
- features_grad: bfloat16 [8, 1500, 768], P('dp', 'tensor')
- w_query_grad: float32 [768, 768], P(None, 'tensor')
- bias_query_grad: float32 [768], P('tensor')
- w_key_grad: float32 [768, 768], P(None, 'tensor')
- w_value_grad: float32 [768, 768], P(None, 'tensor')
- bias_value_grad: float32 [768], P('tensor')
- w_out_grad: float32 [768, 768], P('tensor')
- bias_out_grad: float32 [768], replicated
- norm1_gain_grad: float32 [768], replicated
- norm1_bias_grad: float32 [768], replicated
- norm2_gain_grad: float32 [768], replicated
- norm2_bias_grad: float32 [768], replicated
- w_fc1_grad: float32 [768, 3072], P(None, 'tensor')
- bias_fc1_grad: float32 [3072], P('tensor')
- w_fc2_grad: float32 [3072, 768], P('tensor')
- bias_fc2_grad: float32 [768], replicated
All inputs are finite; a program needn't handle non-finite values.
Results may differ from a plain program's by a relative error of at most 0.015.
Values may be sent and summed in bfloat16 or wider, within the bound.
No kernel may reach another device: no remote copies, remote signals or barrier semaphores. Data moves between devices by JAX's collectives and lax.ppermute only.
A program may use at most 192 MiB of HBM per device.

v0:
```python
import jax
import jax.numpy as jnp
from jax import lax
from jax.sharding import PartitionSpec as P

HEAD_DIM = 64


def normalize(values, gain, shift):
    mean = jnp.mean(values, axis=-1, keepdims=True)
    centred = values - mean
    spread = jnp.mean(centred * centred, axis=-1, keepdims=True)
    scaler = lax.rsqrt(spread + 1e-05)
    unit = centred * scaler
    return (unit * gain + shift, unit, scaler)


def normalize_back(grad_out, unit, scaler, gain):
    scaled = grad_out * gain
    grad_in = scaler * (
        scaled
        - jnp.mean(scaled, axis=-1, keepdims=True)
        - unit * jnp.mean(scaled * unit, axis=-1, keepdims=True)
    )
    return (grad_in, jnp.sum(grad_out * unit, axis=(0, 1)), jnp.sum(grad_out, axis=(0, 1)))


def attend(block):
    query, key, value = block
    scale = query.shape[-1] ** (-0.5)
    scores = jnp.einsum("qhd,khd->hqk", query, key, preferred_element_type=jnp.float32) * scale
    top = jnp.max(scores, axis=-1, keepdims=True)
    weights = jnp.exp(scores - top)
    total = jnp.sum(weights, axis=-1, keepdims=True)
    probs = (weights / total).astype(jnp.bfloat16)
    mixed = jnp.einsum("hqk,khd->qhd", probs, value, preferred_element_type=jnp.float32)
    return (mixed.astype(jnp.bfloat16), (top + jnp.log(total))[..., 0])


def attend_back(block):
    query, key, value, mixed_grad, logsum = block
    scale = query.shape[-1] ** (-0.5)
    scores = jnp.einsum("qhd,khd->hqk", query, key, preferred_element_type=jnp.float32) * scale
    probs = jnp.exp(scores - logsum[..., None])
    value_grad = jnp.einsum(
        "hqk,qhd->khd", probs.astype(jnp.bfloat16), mixed_grad, preferred_element_type=jnp.float32
    )
    prob_grad = jnp.einsum("qhd,khd->hqk", mixed_grad, value, preferred_element_type=jnp.float32)
    delta = jnp.sum(prob_grad * probs, axis=-1, keepdims=True)
    score_grad = (probs * (prob_grad - delta)).astype(jnp.bfloat16)
    query_grad = (
        jnp.einsum("hqk,khd->qhd", score_grad, key, preferred_element_type=jnp.float32) * scale
    )
    key_grad = (
        jnp.einsum("hqk,qhd->khd", score_grad, query, preferred_element_type=jnp.float32) * scale
    )
    return (
        query_grad.astype(jnp.bfloat16),
        key_grad.astype(jnp.bfloat16),
        value_grad.astype(jnp.bfloat16),
    )


def on_device(
    features,
    cotangent,
    w_query,
    bias_query,
    w_key,
    w_value,
    bias_value,
    w_out,
    bias_out,
    norm1_gain,
    norm1_bias,
    norm2_gain,
    norm2_bias,
    w_fc1,
    bias_fc1,
    w_fc2,
    bias_fc2,
):
    clips, share, width = features.shape
    local = w_query.shape[1]
    heads_here = local // HEAD_DIM
    inputs = features.astype(jnp.float32)
    normed1, unit1, scaler1 = normalize(inputs, norm1_gain, norm1_bias)
    rows_one = lax.all_gather(normed1.astype(jnp.bfloat16), "tensor", axis=1, tiled=True)
    frames = rows_one.shape[1]
    w_stack = jnp.concatenate([w_query, w_key, w_value], axis=1)
    project = jnp.einsum("ctd,de->cte", rows_one, w_stack, preferred_element_type=jnp.float32)
    head_shape = (clips, frames, heads_here, HEAD_DIM)
    query = (project[..., :local] + bias_query).astype(jnp.bfloat16).reshape(head_shape)
    key = project[..., local : 2 * local].astype(jnp.bfloat16).reshape(head_shape)
    value = (project[..., 2 * local :] + bias_value).astype(jnp.bfloat16).reshape(head_shape)
    mixed, logsum = lax.map(attend, (query, key, value))
    mixed_flat = mixed.reshape(clips, frames, local)
    branch = jnp.einsum("cte,ed->ctd", mixed_flat, w_out, preferred_element_type=jnp.float32)
    hidden1 = (
        inputs + lax.psum_scatter(branch, "tensor", scatter_dimension=1, tiled=True) + bias_out
    )
    normed2, unit2, scaler2 = normalize(hidden1, norm2_gain, norm2_bias)
    rows_two = lax.all_gather(normed2.astype(jnp.bfloat16), "tensor", axis=1, tiled=True)
    pre = jnp.einsum("ctd,df->ctf", rows_two, w_fc1, preferred_element_type=jnp.float32) + bias_fc1
    active, gelu_back = jax.vjp(lambda t: jax.nn.gelu(t, approximate=False), pre)
    active_low = active.astype(jnp.bfloat16)
    mlp_part = jnp.einsum("ctf,fd->ctd", active_low, w_fc2, preferred_element_type=jnp.float32)
    layer_out = (
        hidden1
        + lax.psum_scatter(
            mlp_part.astype(jnp.bfloat16), "tensor", scatter_dimension=1, tiled=True
        ).astype(jnp.float32)
        + bias_fc2
    ).astype(jnp.bfloat16)
    grad_out = cotangent.astype(jnp.float32)
    fc2_bias_grad = jnp.sum(grad_out, axis=(0, 1))
    grad_rows = lax.all_gather(cotangent, "tensor", axis=1, tiled=True)
    fc2_grad = jnp.einsum("ctf,ctd->fd", active_low, grad_rows, preferred_element_type=jnp.float32)
    active_grad = jnp.einsum("ctd,fd->ctf", grad_rows, w_fc2, preferred_element_type=jnp.float32)
    (pre_grad,) = gelu_back(active_grad)
    fc1_bias_grad = jnp.sum(pre_grad, axis=(0, 1))
    pre_low = pre_grad.astype(jnp.bfloat16)
    fc1_grad = jnp.einsum("ctd,ctf->df", rows_two, pre_low, preferred_element_type=jnp.float32)
    normed2_part = jnp.einsum("ctf,df->ctd", pre_low, w_fc1, preferred_element_type=jnp.float32)
    normed2_grad = lax.psum_scatter(normed2_part, "tensor", scatter_dimension=1, tiled=True)
    hidden_back, gain2_grad, shift2_grad = normalize_back(normed2_grad, unit2, scaler2, norm2_gain)
    hidden1_grad = grad_out + hidden_back
    out_bias_grad = jnp.sum(hidden1_grad, axis=(0, 1))
    branch_rows = lax.all_gather(hidden1_grad.astype(jnp.bfloat16), "tensor", axis=1, tiled=True)
    w_out_grad = jnp.einsum(
        "cte,ctd->ed", mixed_flat, branch_rows, preferred_element_type=jnp.float32
    )
    mixed_grad = jnp.einsum("ctd,ed->cte", branch_rows, w_out, preferred_element_type=jnp.float32)
    mixed_grad = mixed_grad.astype(jnp.bfloat16).reshape(head_shape)
    query_grad, key_grad, value_grad = lax.map(attend_back, (query, key, value, mixed_grad, logsum))
    flat_shape = (clips, frames, local)
    query_flat = query_grad.reshape(flat_shape)
    value_flat = value_grad.reshape(flat_shape)
    stack_grad = jnp.concatenate([query_flat, key_grad.reshape(flat_shape), value_flat], axis=-1)
    weights_grad = jnp.einsum(
        "ctd,cte->de", rows_one, stack_grad, preferred_element_type=jnp.float32
    )
    query_bias_grad = jnp.sum(query_flat.astype(jnp.float32), axis=(0, 1))
    value_bias_grad = jnp.sum(value_flat.astype(jnp.float32), axis=(0, 1))
    normed1_part = jnp.einsum(
        "cte,de->ctd", stack_grad, w_stack, preferred_element_type=jnp.float32
    )
    normed1_grad = lax.psum_scatter(
        normed1_part.astype(jnp.bfloat16), "tensor", scatter_dimension=1, tiled=True
    ).astype(jnp.float32)
    input_back, gain1_grad, shift1_grad = normalize_back(normed1_grad, unit1, scaler1, norm1_gain)
    features_grad = (hidden1_grad + input_back).astype(jnp.bfloat16)
    query_w_grad = weights_grad[:, :local]
    key_w_grad = weights_grad[:, local : 2 * local]
    value_w_grad = weights_grad[:, 2 * local :]
    (
        query_w_grad,
        key_w_grad,
        value_w_grad,
        w_out_grad,
        query_bias_grad,
        value_bias_grad,
        fc1_grad,
        fc2_grad,
        fc1_bias_grad,
    ) = lax.psum(
        (
            query_w_grad,
            key_w_grad,
            value_w_grad,
            w_out_grad,
            query_bias_grad,
            value_bias_grad,
            fc1_grad,
            fc2_grad,
            fc1_bias_grad,
        ),
        "dp",
    )
    gain1_grad, shift1_grad, gain2_grad, shift2_grad, out_bias_grad, fc2_bias_grad = lax.psum(
        (gain1_grad, shift1_grad, gain2_grad, shift2_grad, out_bias_grad, fc2_bias_grad),
        ("dp", "tensor"),
    )
    return (
        layer_out,
        features_grad,
        query_w_grad,
        query_bias_grad,
        key_w_grad,
        value_w_grad,
        value_bias_grad,
        w_out_grad,
        out_bias_grad,
        gain1_grad,
        shift1_grad,
        gain2_grad,
        shift2_grad,
        fc1_grad,
        fc1_bias_grad,
        fc2_grad,
        fc2_bias_grad,
    )


def solution(mesh):
    in_specs = (
        P("dp", "tensor", None),
        P("dp", "tensor", None),
        P(None, "tensor"),
        P("tensor"),
        P(None, "tensor"),
        P(None, "tensor"),
        P("tensor"),
        P("tensor", None),
        P(),
        P(),
        P(),
        P(),
        P(),
        P(None, "tensor"),
        P("tensor"),
        P("tensor", None),
        P(),
    )
    out_specs = (
        P("dp", "tensor", None),
        P("dp", "tensor", None),
        P(None, "tensor"),
        P("tensor"),
        P(None, "tensor"),
        P(None, "tensor"),
        P("tensor"),
        P("tensor", None),
        P(),
        P(),
        P(),
        P(),
        P(),
        P(None, "tensor"),
        P("tensor"),
        P("tensor", None),
        P(),
    )
    return jax.shard_map(
        on_device, mesh=mesh, in_specs=in_specs, out_specs=out_specs, check_vma=False
    )
```

profile of v0, /device:TPU:0, one launch (start us, length us, event | category | flops | bytes accessed | tf_op | source)
XLA Modules:
  0.0 830.7 jit_solution(11836292966475789118)
XLA Ops:
  20.7 39.3 %all-gather.5.cloned.1.call-done = bf16[1,1500,768]{2,0,1:T(2,128)(2,1)} async-done(((bf16[1,375,768]{2,0,1:T(2,128)(2,1)}), bf16[1,1500,768]{2,0,1:T(2,128)(2,1)}) %all-gather.5.cloned.1.call-update) | async-done | bytes 2304016 | tf_op jit(solution)/shard_map/all_gather | solution.py:88
  64.1 11.3 %multiply_reduce_fusion.1 = (f32[3,1500]{1,0:T(4,128)S(1)}, f32[3,1500,1500]{1,2,0:T(8,128)}) fusion(bf16[1500,3,64]{0,2,1:T(8,128)(2,1)S(1)} %bitcast.102, bf16[1500,3,64]{0,2,1:T(8,128)(2,1)S(1)} %bitcast.100), kind=kOutput, calls=%fused_computation.6 | convolution fusion | flops 877495488 | bytes 28170000 | tf_op jit(solution)/shard_map/while/body/eval_jaxpr/qhd,khd->hqk/dot_general | solution.py:31
  75.4 11.8 %fusion.2 = f32[3,1500]{1,0:T(4,128)S(1)} fusion(f32[3,1500,1500]{1,2,0:T(8,128)} %get-tuple-element.144, f32[3,1500]{1,0:T(4,128)S(1)} %get-tuple-element.143), kind=kLoop, calls=%fused_computation.5 | loop fusion | flops 20245500 | bytes 27036000 | tf_op jit(solution)/shard_map/while/body/eval_jaxpr/reduce_sum | solution.py:34
  87.2 11.6 %fusion.17 = bf16[3,64,1500]{2,1,0:T(8,128)(2,1)S(1)} fusion(bf16[1500,3,64]{0,2,1:T(8,128)(2,1)S(1)} %bitcast.108, f32[3,1500,1500]{1,2,0:T(8,128)} %get-tuple-element.144, f32[3,1500]{1,0:T(4,128)S(1)} %fusion.2, f32[3,1500]{1,0:T(4,128)S(1)} %get-tuple-element.143), kind=kOutput, calls=%fused_computation.39 | convolution fusion | flops 891288000 | bytes 28188000 | tf_op jit(solution)/shard_map/while/body/eval_jaxpr/hqk,khd->qhd/dot_general | solution.py:36
  99.7 25.8 %copy.53 = f32[1,1500,768]{2,0,1:T(1,128)} copy(f32[1,1500,768]{2,1,0:T(8,128)S(1)} %convolution_bitcast_fusion.1) | data formatting | bytes 9216000 | tf_op jit(solution)/shard_map/cte,ed->ctd/dot_general | solution.py:98
  127.4 90.6 %all-reduce.14.cloned.1.call-done = f32[1,1500,768]{2,0,1:T(1,128)} async-done(((f32[1,1500,768]{2,0,1:T(1,128)}), f32[1,1500,768]{2,0,1:T(1,128)}) %all-reduce.14.cloned.1.call-update) | async-done | bytes 4608016
  234.2 33.3 %all-gather.7.cloned.1.call-done = bf16[1,1500,768]{2,0,1:T(2,128)(2,1)} async-done(((bf16[1,375,768]{2,0,1:T(2,128)(2,1)}), bf16[1,1500,768]{2,0,1:T(2,128)(2,1)}) %all-gather.7.cloned.1.call-update) | async-done | bytes 2304016 | tf_op jit(solution)/shard_map/all_gather | solution.py:103
  267.5 15.0 %multiply_convert_fusion.1 = (bf16[1500,768]{1,0:T(8,128)(2,1)}, f32[1500,768]{1,0:T(8,128)}, f32[1500,768]{1,0:T(8,128)}) fusion(f32[768]{0:T(1024)} %convert_element_type.129, bf16[768,768]{1,0:T(8,128)(2,1)S(1)} %copy-done, bf16[1,1500,768]{2,0,1:T(2,128)(2,1)} %all-gather.7.cloned.1.call-done), kind=kOutput, calls=%fused_computation.13 | convolution fusion | flops 1845504000 | bytes 15006720 | tf_op jit(solution)/shard_map/ctd,df->ctf/dot_general | solution.py:104
  282.6 23.9 %all-gather.9.cloned.1.call-done = bf16[1,1500,768]{2,0,1:T(2,128)(2,1)} async-done(((bf16[1,375,768]{2,0,1:T(2,128)(2,1)}), bf16[1,1500,768]{2,0,1:T(2,128)(2,1)}) %all-gather.9.cloned.1.call-update) | async-done | bytes 2304016 | tf_op jit(solution)/shard_map/all_gather | solution.py:117
  306.5 9.5 %fusion.71 = (f32[768]{0:T(1024)}, bf16[1500,768]{1,0:T(8,128)(2,1)S(1)}) fusion(f32[1500,768]{1,0:T(8,128)} %get-tuple-element.126, bf16[768,768]{1,0:T(8,128)(2,1)} %param.32, bf16[1,1500,768]{2,0,1:T(2,128)(2,1)} %all-gather.9.cloned.1.call-done, f32[1500,768]{1,0:T(8,128)} %get-tuple-element.145, f32[768]{0:T(1024)} %convert_element_type.129), kind=kOutput, calls=%fused_computation.124 | convolution fusion | flops 1787903232 | bytes 15009792 | tf_op jit(solution)/shard_map/ctd,fd->ctf/dot_general | solution.py:119
  318.0 26.0 %copy.57 = f32[1,1500,768]{2,0,1:T(1,128)} copy(f32[1,1500,768]{2,1,0:T(8,128)S(1)} %convolution_bitcast_fusion) | data formatting | bytes 9216000 | tf_op jit(solution)/shard_map/ctf,df->ctd/dot_general | solution.py:124
  344.1 92.4 %all-reduce.16.cloned.1.call-done = f32[1,1500,768]{2,0,1:T(1,128)} async-done(((f32[1,1500,768]{2,0,1:T(1,128)}), f32[1,1500,768]{2,0,1:T(1,128)}) %all-reduce.16.cloned.1.call-update) | async-done | bytes 4608016
  436.5 7.2 multiply_reduce_fusion.2
  451.9 6.6 fusion.30
  462.1 26.6 %all-gather.11.cloned.1.call-done = bf16[1,1500,768]{2,0,1:T(2,128)(2,1)} async-done(((bf16[1,375,768]{2,0,1:T(2,128)(2,1)}), bf16[1,1500,768]{2,0,1:T(2,128)(2,1)}) %all-gather.11.cloned.1.call-update) | async-done | bytes 2304016 | tf_op jit(solution)/shard_map/all_gather | solution.py:129
  491.9 12.3 %convert_reduce_fusion = (f32[3,64]{1,0:T(4,128)S(1)}, bf16[3,64,1500]{2,1,0:T(8,128)(2,1)}) fusion(bf16[1500,3,64]{0,2,1:T(8,128)(2,1)S(1)} %bitcast.106, f32[3,1500,1500]{1,2,0:T(8,128)} %get-tuple-element.144, f32[3,1500]{1,0:T(4,128)S(1)} %log_add_fusion), kind=kOutput, calls=%fused_computation.61 | convolution fusion | flops 885113792 | bytes 28170768 | tf_op jit(solution)/shard_map/while/body/eval_jaxpr/hqk,qhd->khd/dot_general | solution.py:45
  504.2 21.4 %multiply_reduce_fusion = (f32[3,1500]{1,0:T(4,128)S(1)}, f32[3,1500,1500]{1,2,0:T(8,128)}) fusion(f32[3,1500,1500]{1,2,0:T(8,128)} %get-tuple-element.144, f32[3,1500]{1,0:T(4,128)S(1)} %log_add_fusion, bf16[1500,3,64]{0,2,1:T(8,128)(2,1)S(1)} %bitcast.107, bf16[1500,3,64]{0,2,1:T(8,128)(2,1)S(1)} %bitcast.109), kind=kOutput, calls=%fused_computation.1 | convolution fusion | flops 890995520 | bytes 55188000 | tf_op jit(solution)/shard_map/while/body/eval_jaxpr/qhd,khd->hqk/dot_general | solution.py:48
  525.6 24.0 %multiply_convert_fusion = bf16[3,1500,1500]{1,2,0:T(8,128)(2,1)} fusion(f32[3,1500,1500]{1,2,0:T(8,128)} %get-tuple-element.147, f32[3,1500,1500]{1,2,0:T(8,128)} %get-tuple-element.144, f32[3,1500]{1,0:T(4,128)S(1)} %get-tuple-element.146, f32[3,1500]{1,0:T(4,128)S(1)} %log_add_fusion), kind=kLoop, calls=%fused_computation | loop fusion | flops 33750000 | bytes 67536000 | tf_op jit(solution)/shard_map/while/body/eval_jaxpr/convert_element_type | solution.py:50
  549.7 9.2 %fusion.16 = bf16[3,64,1500]{2,1,0:T(8,128)(2,1)S(1)} fusion(bf16[1500,3,64]{0,2,1:T(8,128)(2,1)S(1)} %bitcast.103, bf16[3,1500,1500]{1,2,0:T(8,128)(2,1)} %multiply_convert_fusion), kind=kOutput, calls=%fused_computation.37 | convolution fusion | flops 864576000 | bytes 14652000 | tf_op jit(solution)/shard_map/while/body/eval_jaxpr/hqk,qhd->khd/dot_general | solution.py:55
  558.9 7.6 convert_reduce_fusion.1
  582.1 43.4 %fusion.63 = (bf16[376,768]{1,0:T(8,128)(2,1)S(1)}, bf16[376,768]{1,0:T(8,128)(2,1)S(1)}) fusion(bf16[1,1500,768]{2,1,0:T(8,128)(2,1)} %fusion.13, bf16[1,1500,768]{2,1,0:T(8,128)(2,1)} %fusion.14), kind=kCustom, calls=%all-reduce-scatter.2 | all-reduce-scatter fusion | flops 2310145 | bytes 5763584
  630.7 24.4 %all-reduce.7 = (f32[192]{0:T(256)}, f32[192]{0:T(256)}, f32[768]{0:T(1024)}) all-reduce(f32[192]{0:T(256)S(1)} %reduce_sum.188, f32[192]{0:T(256)S(1)} %reduce_sum.190, f32[768]{0:T(1024)S(1)} %copy-done.37), channel_id=1, replica_groups=mesh['dp'=8,'tensor'=4] {'dp'}, use_global_device_ids=true, to_apply=%region_17.18 | all-reduce | flops 1152 | bytes 9216 | tf_op jit(solution)/shard_map/psum | solution.py:166
  677.2 38.3 %all-reduce.6 = (f32[768]{0:T(1024)}, f32[768]{0:T(1024)}, f32[768]{0:T(1024)}, f32[768]{0:T(1024)}, f32[768]{0:T(1024)}, /*index=5*/f32[768]{0:T(1024)}) all-reduce(f32[768]{0:T(1024)S(1)} %copy-done.33, f32[768]{0:T(1024)S(1)} %get-tuple-element.100, ...), channel_id=1, replica_groups=mesh['dp'=8,'tensor'=4] {'dp','tensor'}, use_global_device_ids=true, to_apply=%region_24.25 | all-reduce | flops 4608 | bytes 36864 | tf_op jit(solution)/shard_map/psum | solution.py:180
  715.5 97.2 %all-reduce.18.cloned.1.call-done = (f32[768,192]{0,1:T(8,128)}, f32[768,192]{0,1:T(8,128)}, f32[768,192]{0,1:T(8,128)}, f32[192,768]{1,0:T(8,128)}, f32[768,768]{1,0:T(8,128)}, /*index=5*/f32[768,768]{1,0:T(8,128)}) async-done(((f32[768,192]{0,1:T(8,128)}, f32[768,192]{0,1:T(8,128)}, f32[768,192]{0,1:T(8,128)}, f32[192,768]{1,0:T(8,128)}, f32[768,768]{1,0:T(8,128)}, /*index=5*/f32[768,768]{1,0:T(8,128)}), ...) | async-done | bytes 7077904 | tf_op jit(solution)/shard_map/psum | solution.py:166
  (169 shorter events, 105.4 us)
Async XLA Ops:
  7.2 260.3 %copy-start = (bf16[768,768]{1,0:T(8,128)(2,1)S(1)}, bf16[768,768]{1,0:T(8,128)(2,1)}, u32[]{:S(2)}) copy-start(bf16[768,768]{1,0:T(8,128)(2,1)} %param.30) | copy-start | bytes 3538948
  7.3 52.7 %all-gather.5.cloned.1.call-start = ((), (), s32[]{:S(2)}) async-start(), calls=%async_computation | async-start | bytes 5760000 | tf_op jit(solution)/shard_map/all_gather | solution.py:88
  20.3 197.8 %all-reduce.14.cloned.1.call-start = ((), (), s32[]{:S(2)}) async-start(), calls=%async_computation.4 | async-start | bytes 9216000
  20.7 43.2 %copy-start.23 = (bf16[768,576]{0,1:T(8,128)(2,1)}, bf16[768,576]{0,1:T(8,128)(2,1)S(1)}, u32[]{:S(2)}) copy-start(bf16[768,576]{0,1:T(8,128)(2,1)S(1)} %constant_dynamic-update-slice_fusion) | copy-start | bytes 2654212
  64.1 23.1 %copy-start.12 = (bf16[1,1500,192]{1,2,0:T(8,128)(2,1)}, bf16[1,1500,192]{1,2,0:T(8,128)(2,1)S(1)}, u32[]{:S(2)}) copy-start(bf16[1,1500,192]{1,2,0:T(8,128)(2,1)S(1)} %get-tuple-element.136) | copy-start | bytes 1728004
  125.5 92.5 %copy-start.9 = (bf16[1,375,768]{2,1,0:T(8,128)(2,1)S(1)}, bf16[1,375,768]{2,1,0:T(8,128)(2,1)}, u32[]{:S(2)}) copy-start(bf16[1,375,768]{2,1,0:T(8,128)(2,1)} %param.17) | copy-start | bytes 1728004
  125.5 92.5 %copy-start.35 = (f32[768]{0:T(1024)S(1)}, f32[768]{0:T(1024)}, u32[]{:S(2)}) copy-start(f32[768]{0:T(1024)} %param.25) | copy-start | bytes 9220
  125.5 101.2 %copy-start.25 = (f32[768]{0:T(1024)S(1)}, f32[768]{0:T(1024)}, u32[]{:S(2)}) copy-start(f32[768]{0:T(1024)} %param.28) | copy-start | bytes 9220
  125.6 104.9 %copy-start.15 = (bf16[1,375,768]{2,1,0:T(8,128)(2,1)S(1)}, bf16[1,375,768]{2,1,0:T(8,128)(2,1)}, u32[]{:S(2)}) copy-start(bf16[1,375,768]{2,1,0:T(8,128)(2,1)} %param.18) | copy-start | bytes 1728004
  125.6 141.9 %all-gather.7.cloned.1.call-start = ((), (), s32[]{:S(2)}) async-start(), calls=%async_computation.1 | async-start | bytes 5760000 | tf_op jit(solution)/shard_map/all_gather | solution.py:103
  230.5 76.0 %all-gather.9.cloned.1.call-start = ((), (), s32[]{:S(2)}) async-start(), calls=%async_computation.2 | async-start | bytes 5760000 | tf_op jit(solution)/shard_map/all_gather | solution.py:117
  232.4 204.1 %all-reduce.16.cloned.1.call-start = ((), (), s32[]{:S(2)}) async-start(), calls=%async_computation.5 | async-start | bytes 9216000
  344.0 99.7 %copy-start.30 = (f32[375]{0:T(512)S(1)}, f32[375]{0:T(512)}, u32[]{:S(2)}) copy-start(f32[375]{0:T(512)} %copy-done.29) | copy-start | bytes 4504
  344.0 144.6 %all-gather.11.cloned.1.call-start = ((), (), s32[]{:S(2)}) async-start(), calls=%async_computation.3 | async-start | bytes 5760000 | tf_op jit(solution)/shard_map/all_gather | solution.py:129
  451.6 361.0 %all-reduce.18.cloned.1.call-start = ((), (), s32[]{:S(2)}) async-start(), calls=%async_computation.6 | async-start | bytes 14155776 | tf_op jit(solution)/shard_map/psum | solution.py:166
  458.6 30.1 %copy-start.19 = (bf16[192,768]{1,0:T(8,128)(2,1)S(1)}, bf16[192,768]{1,0:T(8,128)(2,1)}, u32[]{:S(2)}) copy-start(bf16[192,768]{1,0:T(8,128)(2,1)} %param.24) | copy-start | bytes 884740
  525.6 24.0 %copy-start.8 = (bf16[1,1500,192]{1,2,0:T(8,128)(2,1)S(1)}, bf16[1,1500,192]{1,2,0:T(8,128)(2,1)}, u32[]{:S(2)}) copy-start(bf16[1,1500,192]{1,2,0:T(8,128)(2,1)} %copy-done.7) | copy-start | bytes 1728004
  582.1 48.6 %copy-start.37 = (f32[768]{0:T(1024)S(1)}, f32[768]{0:T(1024)}, u32[]{:S(2)}) copy-start(f32[768]{0:T(1024)} %get-tuple-element.152) | copy-start | bytes 9220
  582.1 78.4 %copy-start.6 = (f32[1,375,768]{2,0,1:T(1,128)S(1)}, f32[1,375,768]{2,0,1:T(1,128)}, u32[]{:S(2)}) copy-start(f32[1,375,768]{2,0,1:T(1,128)} %get-tuple-element.132) | copy-start | bytes 3456004
  582.1 78.4 %copy-start.26 = (f32[768]{0:T(1024)S(1)}, f32[768]{0:T(1024)}, u32[]{:S(2)}) copy-start(f32[768]{0:T(1024)} %param.26) | copy-start | bytes 9220
  582.1 84.3 %copy-start.28 = (f32[375]{0:T(512)S(1)}, f32[375]{0:T(512)}, u32[]{:S(2)}) copy-start(f32[375]{0:T(512)} %copy-done.27) | copy-start | bytes 4504
  625.6 34.9 %copy-start.14 = (bf16[376,768]{1,0:T(8,128)(2,1)}, bf16[376,768]{1,0:T(8,128)(2,1)S(1)}, u32[]{:S(2)}) copy-start(bf16[376,768]{1,0:T(8,128)(2,1)S(1)} %get-tuple-element.121) | copy-start | bytes 1732612
  625.6 29.5 %collective-permute-start.1 = (bf16[3,768]{1,0:T(4,128)(2,1)S(1)}, bf16[3,768]{1,0:T(4,128)(2,1)S(1)}, u32[]{:S(2)}, u32[]{:S(2)}) collective-permute-start(bf16[3,768]{1,0:T(4,128)(2,1)S(1)} %slice.32), channel_id=1, source_target_pairs={{0,1},{1,2},{2,3},{4,5},{5,6},{6,7},{8,9},{9,10},{10,11},{12,13},{... | collective-permute-start | bytes 13832
  627.7 44.2 %collective-permute-start = (bf16[3,768]{1,0:T(4,128)(2,1)S(1)}, bf16[3,768]{1,0:T(4,128)(2,1)S(1)}, u32[]{:S(2)}, u32[]{:S(2)}) collective-permute-start(bf16[3,768]{1,0:T(4,128)(2,1)S(1)} %slice.31), channel_id=1, source_target_pairs={{0,1},{1,2},{2,3},{4,5},{5,6},{6,7},{8,9},{9,10},{10,11},{12,13},{... | collective-permute-start | bytes 13832
  (32 other events, 288.2 us)
Sparse Core Ops, SparseCore 0:
  20.4 39.5 all-gather.4
  125.7 92.3 all-reduce.13
  230.6 36.9 all-gather.6
  269.6 36.8 all-gather.8
  344.2 92.3 all-reduce.15
  451.7 36.9 all-gather.10
  573.3 239.3 all-reduce.17
where the time goes:
time: 836 us; the launch traced here: 831 us
  waiting for transfers between devices  403 us (48%)
  matrix products  132 us (16%)
  blocking collectives  106 us (13%)
  other arithmetic  89.2 us (11%)
  local copies, waits for them, and re-layouts  77.4 us (9%)
  between operations  16.7 us (2%)
    unnamed x11, waiting for transfers between devices  183 us
    psum x1, waiting for transfers between devices, on_device(): lax.psum((query_w_grad, key_w_grad, value_w_grad, w_out_grad, query_bias_...  97.2 us
    unnamed x1, blocking collectives  43.4 us
    all_gather x1, waiting for transfers between devices, on_device(): lax.all_gather(normed1.astype(jnp.bfloat16), 'tensor', axis=1, tiled=True)  39.3 us
    psum x1, blocking collectives, on_device(): lax.psum((gain1_grad, shift1_grad, gain2_grad, shift2_grad, out_bias_grad...  38.3 us
    all_gather x1, waiting for transfers between devices, on_device(): lax.all_gather(normed2.astype(jnp.bfloat16), 'tensor', axis=1, tiled=True)  33.3 us
    all_gather x1, waiting for transfers between devices, on_device(): lax.all_gather(hidden1_grad.astype(jnp.bfloat16), 'tensor', axis=1, tiled...  26.6 us
    dot_general x1, local copies, waits for them, and re-layouts, on_device(): jnp.einsum('ctf,df->ctd', pre_low, w_fc1, preferred_element_type=jnp.floa...  26 us
  transfers between devices with their start and end apart: 9, of which 7 were waited for; matrix products, arithmetic and copies ran while one was open for 12% of the time, Pallas kernels for 0%

commit v1 on v0

v1 whole, which is shorter than its diff:
```python
import functools

import jax
import jax.numpy as jnp
from jax import lax
from jax.experimental import pallas as pl
from jax.experimental.pallas import tpu as pltpu
from jax.sharding import PartitionSpec as P

HEAD_DIM = 64
LANES = 128
F32 = jnp.float32
LOW = jnp.bfloat16
MASK = -1e30
CORE, CHIP = 1, 2
ROOM = 56 * 1024 * 1024
NT = (((1,), (1,)), ((), ()))


def params(steps=0):
    semantics = ("arbitrary",) * steps if steps else None
    return pltpu.CompilerParams(vmem_limit_bytes=ROOM, dimension_semantics=semantics)


def cost(flops, moved, exps=0):
    return pl.CostEstimate(flops=flops, bytes_accessed=moved, transcendentals=exps)


def whole(shape):
    return pl.BlockSpec(shape, lambda *_: (0,) * len(shape))


def swap(value, partner):
    size = lax.axis_size("tensor")
    return lax.ppermute(value, "tensor", [(i, i ^ partner) for i in range(size)])


def gather(own):
    across = swap(own, CHIP)
    beside = swap(own, CORE)
    return [own, beside, across, swap(across, CORE)]


def scatter(parts):
    far = parts[2] + swap(parts[3], CORE)
    far = swap(far, CHIP)
    return parts[0], swap(parts[1], CORE), far


def thirds(value):
    high = value.astype(LOW)
    rest = value - high.astype(F32)
    mid = rest.astype(LOW)
    return high, mid, (rest - mid.astype(F32)).astype(LOW)


def place(base, lane, first, pieces):
    for offset, piece in enumerate(pieces):
        base = jnp.where(lane == first + offset, piece, base)
    return base


def norm(values):
    mean = jnp.mean(values, axis=-1, keepdims=True)
    centred = values - mean
    spread = jnp.mean(centred * centred, axis=-1, keepdims=True)
    scaler = lax.rsqrt(spread + 1e-05)
    return centred * scaler, scaler


def norm_back(grad, unit, scaler, gain):
    scaled = grad * gain
    return scaler * (
        scaled
        - jnp.mean(scaled, axis=-1, keepdims=True)
        - unit * jnp.mean(scaled * unit, axis=-1, keepdims=True)
    )


def project_kernel(share, x_ref, gain_ref, shift_ref, w_ref, bias_ref, n_ref, q_ref, k_ref, v_ref):
    unit, _ = norm(x_ref[...].astype(F32))
    normed = (unit * gain_ref[...] + shift_ref[...]).astype(LOW)
    n_ref[...] = normed
    out = jnp.dot(normed, w_ref[...], preferred_element_type=F32) + bias_ref[...]
    heads = q_ref.shape[0]
    row = lax.broadcasted_iota(jnp.int32, (out.shape[0], LANES), 0)
    lane = lax.broadcasted_iota(jnp.int32, (out.shape[0], LANES), 1)
    absent = (row >= share) & (lane == HEAD_DIM)
    scale = HEAD_DIM ** (-0.5)
    for head in range(heads):
        part = lambda which: out[:, (which * heads + head) * LANES :][:, :LANES]
        q_ref[head] = (part(0).astype(LOW).astype(F32) * scale).astype(LOW)
        k_ref[head] = jnp.where(absent, MASK, part(1)).astype(LOW)
        v_ref[head] = part(2).astype(LOW)


def attend_kernel(qa_ref, qb_ref, k_ref, v_ref, o_ref, qa_out, qb_out):
    heads, block, _ = qa_ref.shape
    lane = lax.broadcasted_iota(jnp.int32, (block, LANES), 1)
    for half, (q_ref, q_out) in enumerate(((qa_ref, qa_out), (qb_ref, qb_out))):
        for head in range(heads):
            query = q_ref[head]
            scores = lax.dot_general(query, k_ref[head], NT, preferred_element_type=F32)
            top = jnp.max(scores, axis=-1, keepdims=True)
            weights = jnp.exp(scores - top).astype(LOW)
            out = jnp.dot(weights, v_ref[head], preferred_element_type=F32)
            total = out[:, HEAD_DIM : HEAD_DIM + 1]
            at = (half * heads + head) * HEAD_DIM
            o_ref[:, at : at + HEAD_DIM] = (out / total)[:, :HEAD_DIM].astype(LOW)
            logsum = top + jnp.log(total)
            q_out[head] = place(query, lane, HEAD_DIM + 1, thirds(-logsum))


def feed_kernel(
    x_ref, m_ref, wo_ref, bo_ref, gain_ref, shift_ref, w1_ref, b1_ref, w2_ref, g_ref,
    h_ref, n_ref, a_ref, p_ref, d_ref, db_ref,
):
    step = pl.program_id(0)
    branch = jnp.dot(m_ref[...], wo_ref[...], preferred_element_type=F32)
    hidden = x_ref[...].astype(F32) + branch + bo_ref[...]

    @pl.when(step == 0)
    def _():
        h_ref[...] = hidden
        db_ref[...] = jnp.zeros_like(db_ref)

    unit, _ = norm(hidden)
    normed = (unit * gain_ref[...] + shift_ref[...]).astype(LOW)
    n_ref[...] = normed
    pre = jnp.dot(normed, w1_ref[...], preferred_element_type=F32) + b1_ref[...]
    active_grad = lax.dot_general(g_ref[...], w2_ref[...], NT, preferred_element_type=F32)
    size = jnp.abs(pre)
    bell = jnp.exp(-0.5 * pre * pre)
    t = 1.0 / (1.0 + (0.3275911 * 0.5**0.5) * size)
    poly = t * (
        0.127414796 + t * (-0.142248368 + t * (0.7107068705 + t * (-0.7265760135 + t * 0.5307027145)))
    )
    tail = poly * bell
    gate = jnp.where(pre >= 0, 1.0 - tail, tail)
    a_ref[...] = (pre * gate).astype(LOW)
    pre_grad = active_grad * (gate + pre * bell * 0.3989422804014327)
    db_ref[...] += jnp.sum(pre_grad, axis=0, keepdims=True)
    pre_low = pre_grad.astype(LOW)
    p_ref[...] = pre_low
    d_ref[...] = lax.dot_general(pre_low, w1_ref[...], NT, preferred_element_type=F32).astype(LOW)


def middle_kernel(h_ref, d0_ref, d1_ref, d2_ref, g_ref, gain_ref, out_ref, low_ref, sums_ref):
    grad = d0_ref[...].astype(F32) + d1_ref[...].astype(F32) + d2_ref[...].astype(F32)
    unit, scaler = norm(h_ref[...])
    cot = g_ref[...].astype(F32)
    hidden_grad = cot + norm_back(grad, unit, scaler, gain_ref[...])
    out_ref[...] = hidden_grad
    low_ref[...] = hidden_grad.astype(LOW)
    add = lambda value: jnp.sum(value, axis=0, keepdims=True)
    sums_ref[...] = jnp.concatenate(
        [add(grad * unit), add(grad), add(hidden_grad), add(cot)], axis=0
    )


def attend_back_kernel(
    h_ref, m_ref, q_ref, k_ref, v_ref, wo_ref, dq_ref, dk_ref, dv_ref, kt_ref, dk_sum, dv_sum
):
    step = pl.program_id(0)
    heads, block, _ = q_ref.shape

    @pl.when(step == 0)
    def _():
        dk_sum[...] = jnp.zeros_like(dk_sum)
        dv_sum[...] = jnp.zeros_like(dv_sum)
        for head in range(heads):
            kt_ref[head] = k_ref[head].astype(F32).T[:HEAD_DIM].astype(LOW)

    scale = HEAD_DIM ** (-0.5)
    lane = lax.broadcasted_iota(jnp.int32, (block, LANES), 1)
    mixed_grad = lax.dot_general(
        h_ref[...], wo_ref[...], NT, preferred_element_type=F32
    ).astype(LOW)
    for head in range(heads):
        at = head * HEAD_DIM
        out_grad = mixed_grad[:, head * LANES : (head + 1) * LANES]
        mixed = m_ref[:, at : at + HEAD_DIM].astype(F32)
        delta = jnp.sum(out_grad[:, :HEAD_DIM].astype(F32) * mixed, axis=-1, keepdims=True)
        out_grad = place(out_grad, lane, HEAD_DIM, thirds(-delta))
        query = q_ref[head]
        scores = lax.dot_general(k_ref[head], query, NT, preferred_element_type=F32)
        probs = jnp.exp(scores)
        prob_grad = lax.dot_general(v_ref[head], out_grad, NT, preferred_element_type=F32)
        score_grad = (probs * prob_grad).astype(LOW)
        dv_sum[head] += jnp.dot(probs.astype(LOW), out_grad, preferred_element_type=F32)
        dk_sum[head] += jnp.dot(score_grad, query, preferred_element_type=F32)
        turned = jnp.dot(kt_ref[head], score_grad, preferred_element_type=F32)
        dq_ref[:, at : at + HEAD_DIM] = (turned.T * scale).astype(LOW)

    @pl.when(step == pl.num_programs(0) - 1)
    def _():
        for head in range(heads):
            at = head * HEAD_DIM
            dk_ref[:, at : at + HEAD_DIM] = dk_sum[head][:, :HEAD_DIM].astype(LOW)
            dv_ref[:, at : at + HEAD_DIM] = dv_sum[head][:, :HEAD_DIM].astype(LOW)


def last_kernel(x_ref, d0_ref, d1_ref, d2_ref, h_ref, gain_ref, out_ref, sums_ref):
    share = x_ref.shape[0]
    total = d0_ref[...].astype(F32) + d1_ref[...].astype(F32) + d2_ref[...].astype(F32)
    grad = total[:share]
    unit, scaler = norm(x_ref[...].astype(F32))
    out_ref[...] = (h_ref[...][:share] + norm_back(grad, unit, scaler, gain_ref[...])).astype(LOW)
    add = lambda value: jnp.sum(value, axis=0, keepdims=True)
    sums_ref[...] = jnp.concatenate([add(grad * unit), add(grad)], axis=0)


def on_device(
    features, cotangent, w_query, bias_query, w_key, w_value, bias_value, w_out, bias_out,
    norm1_gain, norm1_bias, norm2_gain, norm2_bias, w_fc1, bias_fc1, w_fc2, bias_fc2,
):
    _, share, width = features.shape
    local = w_query.shape[1]
    heads = local // HEAD_DIM
    hidden = w_fc1.shape[1]
    group = lax.axis_size("tensor")
    rows = -(-share // LANES) * LANES
    frames = group * rows
    block = 256
    row = lambda value: value.astype(F32).reshape(1, -1)
    shape = jax.ShapeDtypeStruct
    x_own, g_own = features[0], cotangent[0]
    fill = ((0, rows - share), (0, 0))
    x_pad, g_pad = jnp.pad(x_own, fill), jnp.pad(g_own, fill)
    x_all = jnp.concatenate(gather(x_pad), axis=0)
    g_all = jnp.concatenate(gather(g_pad), axis=0)
    wo_all = jnp.concatenate(gather(w_out), axis=0)

    tiles = lambda value: jnp.pad(
        value.reshape(-1, heads, HEAD_DIM), ((0, 0), (0, 0), (0, LANES - HEAD_DIM))
    )
    w_tiles = jnp.concatenate([tiles(w_query), tiles(w_key), tiles(w_value)], axis=1)
    w_tiles = w_tiles.reshape(width, 3 * heads * LANES)
    spot = jnp.arange(LANES) - HEAD_DIM
    one_q = jnp.where(spot == 0, HEAD_DIM**0.5, 0.0)
    one_k = jnp.where((spot >= 1) & (spot <= 3), 1.0, 0.0)
    one_v = jnp.where((spot >= 0) & (spot <= 2), 1.0, 0.0)
    bias_tiles = jnp.concatenate(
        [
            tiles(bias_query.astype(F32)) + one_q,
            jnp.broadcast_to(one_k, (1, heads, LANES)),
            tiles(bias_value.astype(F32)) + one_v,
        ],
        axis=1,
    ).reshape(1, 3 * heads * LANES)

    per_rows = lambda n: pl.BlockSpec((rows, n), lambda i: (i, 0))
    head_rows = pl.BlockSpec((heads, rows, LANES), lambda i: (0, i, 0))
    head_shape = shape((heads, frames, LANES), LOW)
    normed1, query, key, value = pl.pallas_call(
        functools.partial(project_kernel, share),
        grid=(group,),
        in_specs=[
            per_rows(width), whole((1, width)), whole((1, width)),
            whole(w_tiles.shape), whole(bias_tiles.shape),
        ],
        out_specs=[per_rows(width), head_rows, head_rows, head_rows],
        out_shape=[shape((frames, width), LOW), head_shape, head_shape, head_shape],
        compiler_params=params(1),
        cost_estimate=cost(2 * frames * width * 9 * LANES, 12_000_000),
        name="project",
    )(x_all, row(norm1_gain), row(norm1_bias), w_tiles, bias_tiles)

    half = frames // 2
    steps = half // block
    head_block = lambda shift: pl.BlockSpec((heads, block, LANES), lambda i: (0, i + shift, 0))
    head_whole = whole((heads, frames, LANES))
    half_shape = shape((heads, half, LANES), LOW)
    mixed, query_a, query_b = pl.pallas_call(
        attend_kernel,
        grid=(steps,),
        in_specs=[head_block(0), head_block(steps), head_whole, head_whole],
        out_specs=[pl.BlockSpec((block, 2 * local), lambda i: (i, 0)), head_block(0), head_block(0)],
        out_shape=[shape((half, 2 * local), LOW), half_shape, half_shape],
        compiler_params=params(1),
        cost_estimate=cost(4 * heads * frames * frames * 256, 5_000_000, heads * frames * frames),
        name="attend",
    )(query, query, key, value)
    query_back = jnp.concatenate([query_a, query_b], axis=1)

    def slot(packed, j):
        return packed[(j % 2) * rows :, (j // 2) * local :][:rows, :local]

    mixed_parts = gather(mixed)
    mixed_own = jnp.concatenate([slot(mixed, j) for j in range(group)], axis=0)
    mixed_all = jnp.concatenate(
        [
            jnp.concatenate([slot(mixed_parts[k], j ^ k) for k in range(group)], axis=1)
            for j in range(group)
        ],
        axis=0,
    )

    low_rows = shape((frames, hidden), LOW)
    hidden1, normed2, active, pre_low, normed2_part, fc1_bias_grad = pl.pallas_call(
        feed_kernel,
        grid=(group,),
        in_specs=[
            per_rows(width), per_rows(width), whole((width, width)), whole((1, width)),
            whole((1, width)), whole((1, width)), whole((width, hidden)), whole((1, hidden)),
            whole((hidden, width)), per_rows(width),
        ],
        out_specs=[
            whole((rows, width)), per_rows(width), per_rows(hidden), per_rows(hidden),
            per_rows(width), whole((1, hidden)),
        ],
        out_shape=[
            shape((rows, width), F32), shape((frames, width), LOW), low_rows, low_rows,
            shape((frames, width), LOW), shape((1, hidden), F32),
        ],
        compiler_params=params(1),
        cost_estimate=cost(8 * frames * width * hidden, 20_000_000, frames * hidden),
        name="feed",
    )(
        x_all, mixed_all, wo_all, row(bias_out), row(norm2_gain), row(norm2_bias),
        w_fc1, row(bias_fc1), w_fc2, g_all,
    )
    split = lambda value: [value[j * rows : (j + 1) * rows] for j in range(group)]
    first, second, third = scatter(split(normed2_part))
    hidden1_grad, hidden1_low, sums2 = pl.pallas_call(
        middle_kernel,
        out_shape=[
            shape((rows, width), F32), shape((rows, width), LOW), shape((4, width), F32),
        ],
        compiler_params=params(),
        cost_estimate=cost(20 * rows * width, 8 * rows * width),
        name="middle",
    )(hidden1, first, second, third, g_pad, row(norm2_gain))
    hidden1_rows = jnp.concatenate(gather(hidden1_low), axis=0)

    mlp_part = jnp.dot(active, w_fc2, preferred_element_type=F32).astype(LOW)
    mlp = [part.astype(F32) for part in scatter(split(mlp_part))]
    layer_out = (hidden1 + (mlp[0] + mlp[1] + mlp[2]) + bias_fc2)[None, :share].astype(LOW)
    tn = lambda left, right: lax.dot_general(
        left, right, (((0,), (0,)), ((), ())), preferred_element_type=F32
    )
    over_clips = lambda value: lax.psum(value.astype(LOW), "dp").astype(F32)
    fc2_grad = over_clips(tn(active, g_all))
    fc1_grad = over_clips(tn(normed2, pre_low))
    w_out_grad = over_clips(tn(mixed_own, hidden1_rows))

    wo_tiles = jnp.pad(
        w_out.reshape(heads, HEAD_DIM, width), ((0, 0), (0, LANES - HEAD_DIM), (0, 0))
    ).reshape(heads * LANES, width)
    by_block = lambda n: pl.BlockSpec((block, n), lambda i: (i, 0))
    query_grad, key_grad, value_grad = pl.pallas_call(
        attend_back_kernel,
        grid=(frames // block,),
        in_specs=[
            by_block(width), by_block(local), head_block(0), head_whole, head_whole,
            whole(wo_tiles.shape),
        ],
        out_specs=[by_block(local), whole((frames, local)), whole((frames, local))],
        out_shape=[shape((frames, local), LOW)] * 3,
        scratch_shapes=[
            pltpu.VMEM((heads, HEAD_DIM, frames), LOW),
            pltpu.VMEM((heads, frames, LANES), F32),
            pltpu.VMEM((heads, frames, LANES), F32),
        ],
        compiler_params=params(1),
        cost_estimate=cost(10 * heads * frames * frames * 256, 9_000_000, heads * frames * frames),
        name="attend_back",
    )(hidden1_rows, mixed_own, query_back, key, value, wo_tiles)

    stack_grad = jnp.concatenate([query_grad, key_grad, value_grad], axis=1)
    w_stack = jnp.concatenate([w_query, w_key, w_value], axis=1)
    normed1_part = lax.dot_general(stack_grad, w_stack, NT, preferred_element_type=F32).astype(LOW)
    first, second, third = scatter(split(normed1_part))
    features_grad, sums1 = pl.pallas_call(
        last_kernel,
        out_shape=[shape((share, width), LOW), shape((2, width), F32)],
        compiler_params=params(),
        cost_estimate=cost(20 * rows * width, 8 * rows * width),
        name="last",
    )(x_own, first, second, third, hidden1_grad, row(norm1_gain))

    weights_grad = over_clips(tn(normed1, stack_grad))
    total = jnp.sum(stack_grad.astype(F32), axis=0)
    mine = jnp.concatenate([total[:local], total[2 * local :], fc1_bias_grad[0]])
    spread = jnp.arange(group)[:, None] == lax.axis_index("tensor")
    mine = jnp.where(spread, mine[None], 0.0)
    sums = lax.psum(
        jnp.concatenate([mine.reshape(-1), sums1.reshape(-1), sums2.reshape(-1)]), ("dp", "tensor")
    )
    count = 2 * local + hidden
    mine = lax.dynamic_slice(sums, (lax.axis_index("tensor") * count,), (count,))
    shared = sums[group * count :].reshape(6, width)
    return (
        layer_out,
        features_grad[None],
        weights_grad[:, :local],
        mine[:local],
        weights_grad[:, local : 2 * local],
        weights_grad[:, 2 * local :],
        mine[local : 2 * local],
        w_out_grad,
        shared[4],
        shared[0],
        shared[1],
        shared[2],
        shared[3],
        fc1_grad,
        mine[2 * local :],
        fc2_grad,
        shared[5],
    )


def solution(mesh):
    rows = P("dp", "tensor", None)
    columns, lines, vector, same = P(None, "tensor"), P("tensor", None), P("tensor"), P()
    in_specs = (
        rows, rows, columns, vector, columns, columns, vector, lines, same,
        same, same, same, same, columns, vector, lines, same,
    )
    out_specs = (
        rows, rows, columns, vector, columns, columns, vector, lines, same,
        same, same, same, same, columns, vector, lines, same,
    )
    return jax.shard_map(
        on_device, mesh=mesh, in_specs=in_specs, out_specs=out_specs, check_vma=False
    )
```

time: 836 us -> 369 us (0.44)
  waiting for transfers between devices: 403 us -> 127 us
  matrix products: 132 us -> 17.7 us
  Pallas kernels: 0 us -> 72.6 us
  blocking collectives: 106 us -> 41.7 us
  local copies, waits for them, and re-layouts: 77.4 us -> 21 us
  other arithmetic: 89.2 us -> 51 us
  starting transfers between devices: 5.74 us -> 16.1 us
    unnamed x11 -> x1, waiting for transfers between devices: 183 us -> 0.02 us
    all_gather x4 -> x0, waiting for transfers between devices: 123 us -> none  [the longest x1 39.3 us: on_device(): lax.all_gather(normed1.astype(jnp.bfloat16), 'tensor', axis=1, tiled=True)]
    dot_general x18 -> x6, matrix products: 132 us -> 17.7 us  [the longest x4 13.6 us: on_device(): lax.dot_general(left, right, (((0,), (0,)), ((), ())), preferred_element_...]
    ppermute x0 -> x24, waiting for transfers between devices: none -> 74.5 us  [swap(): lax.ppermute(value, 'tensor', [(i, i ^ partner) for i in range(size)])]
    pallas_call x0 -> x6, Pallas kernels: none -> 72.6 us  [the longest x1 25.3 us: on_device(): pl.pallas_call(attend_back_kernel, grid=(frames // block,), in_specs=[by_...]
    dot_general x2 -> x0, local copies, waits for them, and re-layouts: 51.8 us -> none  [the longest x1 26 us: on_device(): jnp.einsum('ctf,df->ctd', pre_low, w_fc1, preferred_element_type=jnp.floa...]
    reduce_sum x8 -> x1, other arithmetic: 48.7 us -> 0.81 us  [on_device(): total = jnp.sum(stack_grad.astype(F32), axis=0)]
    psum x1, waiting for transfers between devices: 97.2 us -> 52.6 us  [on_device(): over_clips = lambda value: lax.psum(value.astype(LOW), 'dp').astype(F32)]
  transfers between devices with their start and end apart: 9 -> 25, of which waited for: 7 -> 10; matrix products, arithmetic and copies ran while one was open for 12% -> 12% of each run, Pallas kernels for 0% -> 7%
where the time goes in v1:
time: 369 us; the launch traced here: 362 us
  waiting for transfers between devices  127 us (34%)
  Pallas kernels  72.6 us (20%)
  other arithmetic  51 us (14%)
  blocking collectives  41.7 us (11%)
  local copies, waits for them, and re-layouts  21 us (6%)
  matrix products  17.7 us (5%)
  starting transfers between devices  16.1 us (4%)
  between operations  15 us (4%)
    ppermute x24, waiting for transfers between devices, swap(): lax.ppermute(value, 'tensor', [(i, i ^ partner) for i in range(size)])  74.5 us
    psum x1, waiting for transfers between devices, on_device(): over_clips = lambda value: lax.psum(value.astype(LOW), 'dp').astype(F32)  52.6 us
    psum x1, blocking collectives, on_device(): lax.psum(jnp.concatenate([mine.reshape(-1), sums1.reshape(-1), sums2.resh...  41.7 us
    concatenate x1, other arithmetic, on_device(): jnp.concatenate([jnp.concatenate([slot(mixed_parts[k], j ^ k) for k in ra...  26.9 us
    pallas_call x1, Pallas kernels, on_device(): pl.pallas_call(attend_back_kernel, grid=(frames // block,), in_specs=[by_...  25.3 us
    pallas_call x1, Pallas kernels, on_device(): pl.pallas_call(feed_kernel, grid=(group,), in_specs=[per_rows(width), per...  16.9 us
    ppermute x24, starting transfers between devices, swap(): lax.ppermute(value, 'tensor', [(i, i ^ partner) for i in range(size)])  16.1 us
    pallas_call x1, Pallas kernels, on_device(): pl.pallas_call(attend_kernel, grid=(steps,), in_specs=[head_block(0), hea...  14.7 us
  transfers between devices with their start and end apart: 25, of which 10 were waited for; matrix products, arithmetic and copies ran while one was open for 12% of the time, Pallas kernels for 7%

profile of v1, /device:TPU:0, one launch (start us, length us, event | category | flops | bytes accessed | tf_op | source)
XLA Modules:
  0.0 362.3 jit_solution(17635492120778019693)
XLA Ops:
  8.4 3.0 collective-permute-start.1
  16.4 9.3 %collective-permute-done.1 = bf16[384,768]{1,0:T(8,128)(2,1)} collective-permute-done((bf16[384,768]{1,0:T(8,128)(2,1)S(1)}, bf16[384,768]{1,0:T(8,128)(2,1)}, u32[]{:S(2)}, u32[]{:S(2)}) %collective-permute-start.1) | collective-permute-done | bytes 589856 | tf_op jit(solution)/shard_map/ppermute | solution.py:35
  31.0 12.7 %collective-permute-done.7 = bf16[192,768]{1,0:T(8,128)(2,1)S(1)} collective-permute-done((bf16[192,768]{1,0:T(8,128)(2,1)}, bf16[192,768]{1,0:T(8,128)(2,1)S(1)}, u32[]{:S(2)}, u32[]{:S(2)}) %collective-permute-start.7) | collective-permute-done | bytes 294944 | tf_op jit(solution)/shard_map/ppermute | solution.py:35
  44.3 3.0 pad_maximum_fusion.x_ref
  47.3 7.7 %project.1 = (bf16[1536,768]{1,0:T(8,128)(2,1)}, bf16[3,1536,128]{2,1,0:T(8,128)(2,1)}, bf16[3,1536,128]{2,1,0:T(8,128)(2,1)}, bf16[3,1536,128]{2,1,0:T(8,128)(2,1)}) custom-call(bf16[1536,768]{1,0:T(8,128)(2,1)} %pad_maximum_fusion.x_ref, f32[1,768]{1,0:T(1,128)} %reshape.133.gain_ref, f32[1,768]{1,0:T(1,128)} %reshape.134.shift_ref, ...), custom_call_target="tpu_custom_call" | custom-call | flops 2717908992 | bytes 12000000 | tf_op jit(solution)/shard_map/project/pallas_call | solution.py:255
  55.0 14.7 %attend.1 = (bf16[768,384]{1,0:T(8,128)(2,1)}, bf16[3,768,128]{2,1,0:T(8,128)(2,1)}, bf16[3,768,128]{2,1,0:T(8,128)(2,1)}) custom-call(bf16[3,1536,128]{2,1,0:T(8,128)(2,1)} %get-tuple-element.38.qa_ref.qb_ref, bf16[3,1536,128]{2,1,0:T(8,128)(2,1)} %get-tuple-element.38.qa_ref.qb_ref, bf16[3,1536,128]{2,1,0:T(8,128)(2,1)} %get-tuple-element.39.k_ref, ...), custom_call_target="tpu_custom_call" | custom-call | flops 7247757312 | bytes 5000000 | tf_op jit(solution)/shard_map/attend/pallas_call | solution.py:274
  75.1 2.8 pad_maximum_fusion.1.g_ref
  77.9 7.8 %collective-permute-done.4 = bf16[768,384]{1,0:T(8,128)(2,1)S(1)} collective-permute-done((bf16[768,384]{1,0:T(8,128)(2,1)}, bf16[768,384]{1,0:T(8,128)(2,1)S(1)}, u32[]{:S(2)}, u32[]{:S(2)}) %collective-permute-start.4) | collective-permute-done | bytes 589856 | tf_op jit(solution)/shard_map/ppermute | solution.py:35
  87.8 26.9 %maximum_maximum_fusion.m_ref = bf16[1536,768]{1,0:T(8,128)(2,1)} fusion(bf16[384,192]{1,0:T(8,128)(2,1)S(1)} %get-tuple-element.90, bf16[384,192]{1,0:T(8,128)(2,1)S(1)} %get-tuple-element.86, bf16[384,192]{1,0:T(8,128)(2,1)S(1)} %get-tuple-element.82, bf16[384,192]{1,0:T(8,128)(2,1)S(1)} %get-tuple-element.78, bf16[384,192]{1,0:T(8,128)(2,1)S(1)} %get-tuple-element.91, ...), kind=kLoop, calls=%fused_computation.12 | loop fusion | flops 37748736 | bytes 4718592 | tf_op jit(solution)/shard_map/concatenate | solution.py:291
  114.7 16.9 %feed.1 = (f32[384,768]{1,0:T(8,128)}, bf16[1536,768]{1,0:T(8,128)(2,1)}, bf16[1536,768]{1,0:T(8,128)(2,1)}, bf16[1536,768]{1,0:T(8,128)(2,1)}, bf16[1536,768]{1,0:T(8,128)(2,1)}, /*index=5*/f32[1,768]{1,0:T(1,128)}) custom-call(bf16[1536,768]{1,0:T(8,128)(2,1)} %pad_maximum_fusion.x_ref, bf16[1536,768]{1,0:T(8,128)(2,1)} %maximum_maximum_fusion.m_ref, ...), custom_call_target="tpu_custom_call" | custom-call | flops 7247757312 | bytes 20000000 | tf_op jit(solution)/shard_map/feed/pallas_call | solution.py:300
  139.3 3.1 convolution_convert_fusion.3
  142.4 9.5 %collective-permute-done.17.d2_ref = bf16[384,768]{1,0:T(8,128)(2,1)S(1)} collective-permute-done((bf16[384,768]{1,0:T(8,128)(2,1)S(1)}, bf16[384,768]{1,0:T(8,128)(2,1)S(1)}, u32[]{:S(2)}, u32[]{:S(2)}) %collective-permute-start.17) | collective-permute-done | bytes 589856 | tf_op jit(solution)/shard_map/ppermute | solution.py:35
  152.8 4.3 %middle.1 = (f32[384,768]{1,0:T(8,128)}, bf16[384,768]{1,0:T(8,128)(2,1)}, f32[4,768]{1,0:T(4,128)}) custom-call(f32[384,768]{1,0:T(8,128)} %get-tuple-element.42.h_ref, bf16[384,768]{1,0:T(8,128)(2,1)} %get-tuple-element.68.d0_ref, bf16[384,768]{1,0:T(8,128)(2,1)} %copy-done.14, bf16[384,768]{1,0:T(8,128)(2,1)} %copy-done.15, bf16[384,768]{1,0:T(8,128)(2,1)} %copy-done, ...), custom_call_target="tpu_custom_call" | custom-call | flops 5898240 | bytes 2359296 | tf_op jit(solution)/shard_map/middle/pallas_call | solution.py:325
  158.8 4.5 %convolution_convert_fusion.2 = bf16[768,768]{1,0:T(8,128)(2,1)} fusion(bf16[1536,768]{1,0:T(8,128)(2,1)S(1)} %copy-done.38, bf16[384,768]{1,0:T(8,128)(2,1)S(1)} %collective-permute-done.11, bf16[384,768]{1,0:T(8,128)(2,1)} %collective-permute-done.10, bf16[384,768]{1,0:T(8,128)(2,1)} %collective-permute-done.9, bf16[384,768]{1,0:T(8,128)(2,1)S(1)} %copy-done.1), kind=kOutput, calls=%fused_computation.17 | convolution fusion | flops 1821966336 | bytes 5898240 | tf_op jit(solution)/shard_map/dot_general | solution.py:339
  163.3 8.5 %collective-permute-done.19 = bf16[384,768]{1,0:T(8,128)(2,1)S(1)} collective-permute-done((bf16[384,768]{1,0:T(8,128)(2,1)}, bf16[384,768]{1,0:T(8,128)(2,1)S(1)}, u32[]{:S(2)}, u32[]{:S(2)}) %collective-permute-start.19) | collective-permute-done | bytes 589856 | tf_op jit(solution)/shard_map/ppermute | solution.py:35
  175.6 25.3 %attend_back.1 = (bf16[1536,192]{1,0:T(8,128)(2,1)}, bf16[1536,192]{1,0:T(8,128)(2,1)}, bf16[1536,192]{1,0:T(8,128)(2,1)}) custom-call(bf16[1536,768]{1,0:T(8,128)(2,1)} %copy-done.26, bf16[1536,192]{1,0:T(8,128)(2,1)} %pad_maximum_fusion.5.m_ref, bf16[3,1536,128]{2,1,0:T(8,128)(2,1)} %pad_maximum_fusion.4.q_ref, ...), custom_call_target="tpu_custom_call" | custom-call | flops 18119393280 | bytes 9000000 | tf_op jit(solution)/shard_map/attend_back/pallas_call | solution.py:351
  200.8 4.5 %convolution_convert_fusion.4 = bf16[768,576]{0,1:T(8,128)(2,1)} fusion(bf16[1536,768]{1,0:T(8,128)(2,1)S(1)} %copy-done.37, bf16[1536,192]{1,0:T(8,128)(2,1)} %get-tuple-element.50, bf16[1536,192]{1,0:T(8,128)(2,1)} %get-tuple-element.49, bf16[1536,192]{1,0:T(8,128)(2,1)} %get-tuple-element.48), kind=kOutput, calls=%fused_computation.19 | convolution fusion | flops 1364705280 | bytes 5013504 | tf_op jit(solution)/shard_map/dot_general | solution.py:339
  216.4 9.8 %collective-permute-done.14 = bf16[384,768]{1,0:T(8,128)(2,1)} collective-permute-done((bf16[384,768]{1,0:T(8,128)(2,1)}, bf16[384,768]{1,0:T(8,128)(2,1)}, u32[]{:S(2)}, u32[]{:S(2)}) %collective-permute-start.14) | collective-permute-done | bytes 589856 | tf_op jit(solution)/shard_map/ppermute | solution.py:35
  226.2 2.5 fusion.13
  234.2 13.1 %collective-permute-done.23.d2_ref = bf16[384,768]{1,0:T(8,128)(2,1)S(1)} collective-permute-done((bf16[384,768]{1,0:T(8,128)(2,1)S(1)}, bf16[384,768]{1,0:T(8,128)(2,1)S(1)}, u32[]{:S(2)}, u32[]{:S(2)}) %collective-permute-start.23) | collective-permute-done | bytes 589856 | tf_op jit(solution)/shard_map/ppermute | solution.py:35
  248.2 3.9 %last.1 = (bf16[375,768]{1,0:T(8,128)(2,1)}, f32[2,768]{1,0:T(2,128)}) custom-call(bf16[375,768]{1,0:T(8,128)(2,1)} %bitcast.25, bf16[384,768]{1,0:T(8,128)(2,1)} %get-tuple-element.65.d0_ref, bf16[384,768]{1,0:T(8,128)(2,1)} %copy-done.19, bf16[384,768]{1,0:T(8,128)(2,1)} %copy-done.20, f32[384,768]{1,0:T(8,128)} %get-tuple-element.51.h_ref, ...), custom_call_target="tpu_custom_call" | custom-call | flops 5898240 | bytes 2359296 | tf_op jit(solution)/shard_map/last/pallas_call | solution.py:374
  252.7 41.7 %psum.36 = f32[9216]{0:T(1024)S(1)} all-reduce(f32[9216]{0:T(1024)S(1)} %pad_maximum_fusion.6), channel_id=1, replica_groups=mesh['dp'=8,'tensor'=4] {'dp','tensor'}, use_global_device_ids=true, to_apply=%region_2.3 | all-reduce | flops 9216 | bytes 73728 | tf_op jit(solution)/shard_map/psum | solution.py:387
  295.8 52.6 %all-reduce.11.cloned.1.call-done = (bf16[768,576]{0,1:T(8,128)(2,1)}, bf16[192,768]{1,0:T(8,128)(2,1)}, bf16[768,768]{1,0:T(8,128)(2,1)}, bf16[768,768]{1,0:T(8,128)(2,1)}) async-done(((bf16[768,576]{0,1:T(8,128)(2,1)}, bf16[192,768]{1,0:T(8,128)(2,1)}, bf16[768,768]{1,0:T(8,128)(2,1)}, bf16[768,768]{1,0:T(8,128)(2,1)}), (bf16[768,576]{0,1:T(8,128)(2,1)}, bf16[192,768]{1,0:T(8,128)(2,1)}, ...) | async-done | bytes 3538960 | tf_op jit(solution)/shard_map/psum | solution.py:342
  348.4 2.9 convert_element_type.73
  (178 shorter events, 56.2 us)
Async XLA Ops:
  7.2 341.1 %all-reduce.11.cloned.1.call-start = ((), (), s32[]{:S(2)}) async-start(), calls=%async_computation | async-start | bytes 7077888 | tf_op jit(solution)/shard_map/psum | solution.py:342
  8.4 17.3 %collective-permute-start.1 = (bf16[384,768]{1,0:T(8,128)(2,1)S(1)}, bf16[384,768]{1,0:T(8,128)(2,1)}, u32[]{:S(2)}, u32[]{:S(2)}) collective-permute-start(bf16[384,768]{1,0:T(8,128)(2,1)S(1)} %pad.34), channel_id=1, source_target_pairs={{0,2},{1,3},{2,0},{3,1},{4,6},{5,7},{6,4},{7,5},{8,10},{9,11},{10,... | collective-permute-start | bytes 1769480 | tf_op jit(solution)/shard_map/ppermute | solution.py:35
  11.4 32.3 %collective-permute-start = (bf16[384,768]{1,0:T(8,128)(2,1)S(1)}, bf16[384,768]{1,0:T(8,128)(2,1)}, u32[]{:S(2)}, u32[]{:S(2)}) collective-permute-start(bf16[384,768]{1,0:T(8,128)(2,1)S(1)} %pad.34), channel_id=1, source_target_pairs={{0,1},{1,0},{2,3},{3,2},{4,5},{5,4},{6,7},{7,6},{8,9},{9,8},{10,11... | collective-permute-start | bytes 1769480 | tf_op jit(solution)/shard_map/ppermute | solution.py:35
  12.5 31.7 %collective-permute-start.10 = (bf16[384,768]{1,0:T(8,128)(2,1)S(1)}, bf16[384,768]{1,0:T(8,128)(2,1)}, u32[]{:S(2)}, u32[]{:S(2)}) collective-permute-start(bf16[384,768]{1,0:T(8,128)(2,1)S(1)} %pad.42.g_ref), channel_id=1, source_target_pairs={{0,2},{1,3},{2,0},{3,1},{4,6},{5,7},{6,4},{7,5},{8,10},{9,11},{10,... | collective-permute-start | bytes 1769480 | tf_op jit(solution)/shard_map/ppermute | solution.py:35
  12.7 62.4 %collective-permute-start.9 = (bf16[384,768]{1,0:T(8,128)(2,1)S(1)}, bf16[384,768]{1,0:T(8,128)(2,1)}, u32[]{:S(2)}, u32[]{:S(2)}) collective-permute-start(bf16[384,768]{1,0:T(8,128)(2,1)S(1)} %pad.42.g_ref), channel_id=1, source_target_pairs={{0,1},{1,0},{2,3},{3,2},{4,5},{5,4},{6,7},{7,6},{8,9},{9,8},{10,11... | collective-permute-start | bytes 1769480 | tf_op jit(solution)/shard_map/ppermute | solution.py:35
  13.2 30.5 %collective-permute-start.7 = (bf16[192,768]{1,0:T(8,128)(2,1)}, bf16[192,768]{1,0:T(8,128)(2,1)S(1)}, u32[]{:S(2)}, u32[]{:S(2)}) collective-permute-start(bf16[192,768]{1,0:T(8,128)(2,1)} %param.24), channel_id=1, source_target_pairs={{0,2},{1,3},{2,0},{3,1},{4,6},{5,7},{6,4},{7,5},{8,10},{9,11},{10,... | collective-permute-start | bytes 884744 | tf_op jit(solution)/shard_map/ppermute | solution.py:35
  25.7 18.6 %collective-permute-start.2 = (bf16[384,768]{1,0:T(8,128)(2,1)}, bf16[384,768]{1,0:T(8,128)(2,1)}, u32[]{:S(2)}, u32[]{:S(2)}) collective-permute-start(bf16[384,768]{1,0:T(8,128)(2,1)} %collective-permute-done.1), channel_id=1, source_target_pairs={{0,1},{1,0},{2,3},{3,2},{4,5},{5,4},{6,7},{7,6},{8,9},{9,8},{10,11... | collective-permute-start | bytes 1769480 | tf_op jit(solution)/shard_map/ppermute | solution.py:35
  43.7 30.1 %collective-permute-start.6 = (bf16[192,768]{1,0:T(8,128)(2,1)S(1)}, bf16[192,768]{1,0:T(8,128)(2,1)S(1)}, u32[]{:S(2)}, u32[]{:S(2)}) collective-permute-start(bf16[192,768]{1,0:T(8,128)(2,1)S(1)} %copy-done.6), channel_id=1, source_target_pairs={{0,1},{1,0},{2,3},{3,2},{4,5},{5,4},{6,7},{7,6},{8,9},{9,8},{10,11... | collective-permute-start | bytes 884744 | tf_op jit(solution)/shard_map/ppermute | solution.py:35
  43.7 30.1 %collective-permute-start.8 = (bf16[192,768]{1,0:T(8,128)(2,1)S(1)}, bf16[192,768]{1,0:T(8,128)(2,1)S(1)}, u32[]{:S(2)}, u32[]{:S(2)}) collective-permute-start(bf16[192,768]{1,0:T(8,128)(2,1)S(1)} %collective-permute-done.7), channel_id=1, source_target_pairs={{0,1},{1,0},{2,3},{3,2},{4,5},{5,4},{6,7},{7,6},{8,9},{9,8},{10,11... | collective-permute-start | bytes 884744 | tf_op jit(solution)/shard_map/ppermute | solution.py:35
  44.2 30.9 %collective-permute-start.11 = (bf16[384,768]{1,0:T(8,128)(2,1)}, bf16[384,768]{1,0:T(8,128)(2,1)S(1)}, u32[]{:S(2)}, u32[]{:S(2)}) collective-permute-start(bf16[384,768]{1,0:T(8,128)(2,1)} %collective-permute-done.10), channel_id=1, source_target_pairs={{0,1},{1,0},{2,3},{3,2},{4,5},{5,4},{6,7},{7,6},{8,9},{9,8},{10,11... | collective-permute-start | bytes 1769480 | tf_op jit(solution)/shard_map/ppermute | solution.py:35
  69.7 16.0 %collective-permute-start.4 = (bf16[768,384]{1,0:T(8,128)(2,1)}, bf16[768,384]{1,0:T(8,128)(2,1)S(1)}, u32[]{:S(2)}, u32[]{:S(2)}) collective-permute-start(bf16[768,384]{1,0:T(8,128)(2,1)} %get-tuple-element.41), channel_id=1, source_target_pairs={{0,2},{1,3},{2,0},{3,1},{4,6},{5,7},{6,4},{7,5},{8,10},{9,11},{10,... | collective-permute-start | bytes 1769480 | tf_op jit(solution)/shard_map/ppermute | solution.py:35
  74.9 11.1 %collective-permute-start.3 = (bf16[768,384]{1,0:T(8,128)(2,1)S(1)}, bf16[768,384]{1,0:T(8,128)(2,1)S(1)}, u32[]{:S(2)}, u32[]{:S(2)}) collective-permute-start(bf16[768,384]{1,0:T(8,128)(2,1)S(1)} %copy-done.3), channel_id=1, source_target_pairs={{0,1},{1,0},{2,3},{3,2},{4,5},{5,4},{6,7},{7,6},{8,9},{9,8},{10,11... | collective-permute-start | bytes 1769480 | tf_op jit(solution)/shard_map/ppermute | solution.py:35
  132.8 2.4 collective-permute-start.16
  136.2 6.2 %collective-permute-start.15 = (bf16[384,768]{1,0:T(8,128)(2,1)S(1)}, bf16[384,768]{1,0:T(8,128)(2,1)S(1)}, u32[]{:S(2)}, u32[]{:S(2)}) collective-permute-start(bf16[384,768]{1,0:T(8,128)(2,1)S(1)} %get-tuple-element.67), channel_id=1, source_target_pairs={{0,1},{1,0},{2,3},{3,2},{4,5},{5,4},{6,7},{7,6},{8,9},{9,8},{10,11... | collective-permute-start | bytes 1769480 | tf_op jit(solution)/shard_map/ppermute | solution.py:35
  136.6 15.4 %collective-permute-start.17 = (bf16[384,768]{1,0:T(8,128)(2,1)S(1)}, bf16[384,768]{1,0:T(8,128)(2,1)S(1)}, u32[]{:S(2)}, u32[]{:S(2)}) collective-permute-start(bf16[384,768]{1,0:T(8,128)(2,1)S(1)} %get-tuple-element.66), channel_id=1, source_target_pairs={{0,2},{1,3},{2,0},{3,1},{4,6},{5,7},{6,4},{7,5},{8,10},{9,11},{10,... | collective-permute-start | bytes 1769480 | tf_op jit(solution)/shard_map/ppermute | solution.py:35
  157.0 14.7 %collective-permute-start.19 = (bf16[384,768]{1,0:T(8,128)(2,1)}, bf16[384,768]{1,0:T(8,128)(2,1)S(1)}, u32[]{:S(2)}, u32[]{:S(2)}) collective-permute-start(bf16[384,768]{1,0:T(8,128)(2,1)} %get-tuple-element.45), channel_id=1, source_target_pairs={{0,2},{1,3},{2,0},{3,1},{4,6},{5,7},{6,4},{7,5},{8,10},{9,11},{10,... | collective-permute-start | bytes 1769480 | tf_op jit(solution)/shard_map/ppermute | solution.py:35
  163.3 10.6 %collective-permute-start.18 = (bf16[384,768]{1,0:T(8,128)(2,1)S(1)}, bf16[384,768]{1,0:T(8,128)(2,1)S(1)}, u32[]{:S(2)}, u32[]{:S(2)}) collective-permute-start(bf16[384,768]{1,0:T(8,128)(2,1)S(1)} %copy-done.16), channel_id=1, source_target_pairs={{0,1},{1,0},{2,3},{3,2},{4,5},{5,4},{6,7},{7,6},{8,9},{9,8},{10,11... | collective-permute-start | bytes 1769480 | tf_op jit(solution)/shard_map/ppermute | solution.py:35
  171.8 2.2 collective-permute-start.20
  206.6 2.7 collective-permute-start.13
  207.0 9.3 %collective-permute-start.12 = (bf16[384,768]{1,0:T(8,128)(2,1)}, bf16[384,768]{1,0:T(8,128)(2,1)}, u32[]{:S(2)}, u32[]{:S(2)}) collective-permute-start(bf16[384,768]{1,0:T(8,128)(2,1)} %get-tuple-element.71), channel_id=1, source_target_pairs={{0,1},{1,0},{2,3},{3,2},{4,5},{5,4},{6,7},{7,6},{8,9},{9,8},{10,11... | collective-permute-start | bytes 1769480 | tf_op jit(solution)/shard_map/ppermute | solution.py:35
  210.1 16.1 %collective-permute-start.14 = (bf16[384,768]{1,0:T(8,128)(2,1)}, bf16[384,768]{1,0:T(8,128)(2,1)}, u32[]{:S(2)}, u32[]{:S(2)}) collective-permute-start(bf16[384,768]{1,0:T(8,128)(2,1)} %slice_add_fusion.2), channel_id=1, source_target_pairs={{0,2},{1,3},{2,0},{3,1},{4,6},{5,7},{6,4},{7,5},{8,10},{9,11},{10,... | collective-permute-start | bytes 1769480 | tf_op jit(solution)/shard_map/ppermute | solution.py:35
  215.0 14.6 %collective-permute-start.22 = (bf16[384,768]{1,0:T(8,128)(2,1)}, bf16[384,768]{1,0:T(8,128)(2,1)}, u32[]{:S(2)}, u32[]{:S(2)}) collective-permute-start(bf16[384,768]{1,0:T(8,128)(2,1)} %slice.239), channel_id=1, source_target_pairs={{0,1},{1,0},{2,3},{3,2},{4,5},{5,4},{6,7},{7,6},{8,9},{9,8},{10,11... | collective-permute-start | bytes 1769480 | tf_op jit(solution)/shard_map/ppermute | solution.py:35
  231.6 2.6 collective-permute-start.21
  231.6 15.7 %collective-permute-start.23 = (bf16[384,768]{1,0:T(8,128)(2,1)S(1)}, bf16[384,768]{1,0:T(8,128)(2,1)S(1)}, u32[]{:S(2)}, u32[]{:S(2)}) collective-permute-start(bf16[384,768]{1,0:T(8,128)(2,1)S(1)} %get-tuple-element.63), channel_id=1, source_target_pairs={{0,2},{1,3},{2,0},{3,1},{4,6},{5,7},{6,4},{7,5},{8,10},{9,11},{10,... | collective-permute-start | bytes 1769480 | tf_op jit(solution)/shard_map/ppermute | solution.py:35
  (41 other events, 430.4 us)
Sparse Core Ops, SparseCore 0:
  205.5 142.8 all-reduce.10
